TPU v7x, 256 devices: a whole 4x4x8 slice. The times are simulated.
256 devices in a mesh: rep: 32 (over x_lo, z, core), tp: 8 (over x_hi, y).
Axes of the slice: x: 4 (x_hi: 2, x_lo: 2; x = x_hi * 2 + x_lo), y: 4, z: 8, core: 2. Of those that a mesh axis runs over, the one named last changes fastest.
Arguments:
- step_index: int32 [1], replicated, may hold values from 0 to 999
- tokens: bfloat16 [32768, 2048], P(('rep', 'tp')), may hold values from -6 to 6
- cotangent: bfloat16 [32768, 2048], P(('rep', 'tp')), may hold values from -6 to 6
- w_query: bfloat16 [32, 2048, 2048], P('rep', None, 'tp'), as said below
- w_key: bfloat16 [32, 2048, 1024], P('rep', None, 'tp'), as said below
- w_value: bfloat16 [32, 2048, 1024], P('rep', None, 'tp'), may hold values from -0.125 to 0.125
- w_out: bfloat16 [32, 2048, 2048], P('rep', 'tp'), may hold values from -0.125 to 0.125
- last_query: bfloat16 [32, 2048, 2048], P('rep', None, 'tp'), may hold values from -0.029907227 to 0.029907227
- last_key: bfloat16 [32, 2048, 1024], P('rep', None, 'tp'), may hold values from -0.029907227 to 0.029907227
- last_value: bfloat16 [32, 2048, 1024], P('rep', None, 'tp'), may hold values from -0.029907227 to 0.029907227
- last_out: bfloat16 [32, 2048, 2048], P('rep', 'tp'), may hold values from -0.029907227 to 0.029907227
- query_gain: float32 [128], replicated, may hold values from 0.5 to 4.5
- key_gain: float32 [128], replicated, may hold values from 0.5 to 4.5
Outputs:
- new_query: bfloat16 [32, 2048, 2048], P('rep', None, 'tp')
- new_key: bfloat16 [32, 2048, 1024], P('rep', None, 'tp')
- new_value: bfloat16 [32, 2048, 1024], P('rep', None, 'tp')
- new_out: bfloat16 [32, 2048, 2048], P('rep', 'tp')
- input_grad: bfloat16 [32768, 2048], P(('rep', 'tp'))
Inputs may be any that keep to these rules, and one draw needn't show every extreme that they name: `w_query`: each entry lies within 4 / sqrt(2048) of zero. `w_key`: each entry lies within 4 / sqrt(2048) of zero.
All inputs are finite; a program needn't handle non-finite values.
Results may differ from a plain program's by a relative error of at most 0.024.
The roundings to bfloat16 on the way count: a program that leaves them out, or rounds other values in their place, can miss the bound.
Values may be sent and summed in bfloat16 or wider, within the bound.
A program may use at most 128 MiB of HBM per device.

v0:
```python
import math

import jax
import jax.numpy as jnp
from jax import lax
from jax.sharding import PartitionSpec as P

EPSILON = 1e-06
MOMENTUM = 0.9
LEARNING_RATE = 0.001
MASKED = -1e30


def shortened(array):

    def short(part):
        return part.astype(jnp.bfloat16) if part.dtype == jnp.float32 else part

    return jax.tree.map(short, array)


def passed_along(array, axis, by):
    peers = lax.axis_size(axis)
    return lax.ppermute(array, axis, [(i, (i + by) % peers) for i in range(peers)])


def product(pattern, left_in, right_in):
    return jnp.einsum(pattern, left_in, right_in, preferred_element_type=jnp.float32)


def rms_rows(values):
    return values * lax.rsqrt(jnp.mean(values * values, axis=-1, keepdims=True) + EPSILON)


def rope_tables(length, head_dim):
    half_dim = head_dim // 2
    inverse = jnp.exp(
        jnp.arange(half_dim, dtype=jnp.float32) * (-2.0 * math.log(1000000.0) / head_dim)
    )
    angles = jnp.arange(length, dtype=jnp.float32)[:, None] * inverse[None, :]
    return (jnp.cos(angles), jnp.sin(angles))


def shape_heads(raw_rows, gain_vec, cosine_table, sine_table):
    length, total_width = raw_rows.shape
    head_dim = gain_vec.shape[0]
    grouped = raw_rows.reshape(length, total_width // head_dim, head_dim)
    grouped = rms_rows(grouped) * gain_vec
    half_dim = head_dim // 2
    first_half = grouped[..., :half_dim]
    second_half = grouped[..., half_dim:]
    cos_part = cosine_table[:, None, :]
    sin_part = sine_table[:, None, :]
    turned = jnp.concatenate(
        [
            first_half * cos_part - second_half * sin_part,
            second_half * cos_part + first_half * sin_part,
        ],
        axis=-1,
    )
    return turned.reshape(length, total_width)


def softmax_rows(query_block, key_heads, offset, score_scale):
    block_len = query_block.shape[0]
    length = key_heads.shape[0]
    scores = product("bkgd,tkd->kgbt", query_block, key_heads) * score_scale
    row_pos = offset + jnp.arange(block_len, dtype=jnp.int32)[:, None]
    col_pos = jnp.arange(length, dtype=jnp.int32)[None, :]
    scores = jnp.where(col_pos <= row_pos, scores, MASKED)
    highest = jnp.max(scores, axis=-1, keepdims=True)
    raised = jnp.exp(scores - highest)
    return raised / jnp.sum(raised, axis=-1, keepdims=True)


def attend(query_rows, key_rows, value_rows, head_dim):
    length = query_rows.shape[0]
    kv_count = key_rows.shape[1] // head_dim
    group_size = query_rows.shape[1] // key_rows.shape[1]
    key_heads = key_rows.reshape(length, kv_count, head_dim)
    value_heads = value_rows.reshape(length, kv_count, head_dim)
    block_len = min(512, length)
    score_scale = head_dim ** (-0.5)
    outputs = []
    for block_at in range(length // block_len):
        offset = block_at * block_len
        query_block = query_rows[offset : offset + block_len].reshape(
            block_len, kv_count, group_size, head_dim
        )
        probability = softmax_rows(query_block, key_heads, offset, score_scale)
        combined = product("kgbt,tkd->bkgd", probability.astype(jnp.bfloat16), value_heads)
        outputs.append(combined.reshape(block_len, -1).astype(jnp.bfloat16))
    return jnp.concatenate(outputs, axis=0)


def attend_back(query_rows, key_rows, value_rows, d_attended, head_dim):
    length = query_rows.shape[0]
    kv_count = key_rows.shape[1] // head_dim
    group_size = query_rows.shape[1] // key_rows.shape[1]
    key_heads = key_rows.reshape(length, kv_count, head_dim)
    value_heads = value_rows.reshape(length, kv_count, head_dim)
    block_len = min(512, length)
    score_scale = head_dim ** (-0.5)
    d_keys = jnp.zeros((length, kv_count, head_dim), jnp.float32)
    d_values = jnp.zeros((length, kv_count, head_dim), jnp.float32)
    query_parts = []
    for block_at in range(length // block_len):
        offset = block_at * block_len
        query_block = query_rows[offset : offset + block_len].reshape(
            block_len, kv_count, group_size, head_dim
        )
        probability = softmax_rows(query_block, key_heads, offset, score_scale)
        upstream = d_attended[offset : offset + block_len].reshape(
            block_len, kv_count, group_size, head_dim
        )
        d_values = d_values + product("kgbt,bkgd->tkd", probability.astype(jnp.bfloat16), upstream)
        d_prob = product("bkgd,tkd->kgbt", upstream, value_heads)
        centred = d_prob - jnp.sum(probability * d_prob, axis=-1, keepdims=True)
        d_scores = (probability * centred * score_scale).astype(jnp.bfloat16)
        query_parts.append(product("kgbt,tkd->bkgd", d_scores, key_heads).reshape(block_len, -1))
        d_keys = d_keys + product("kgbt,bkgd->tkd", d_scores, query_block)
    return (
        jnp.concatenate(query_parts, axis=0),
        d_keys.reshape(length, -1),
        d_values.reshape(length, -1),
    )


def advance(weight, last_step, gradient):
    return (
        weight.astype(jnp.float32)
        + MOMENTUM * last_step.astype(jnp.float32)
        - LEARNING_RATE * gradient
    ).astype(jnp.bfloat16)


def average(own_copy, partner):
    return (0.5 * (own_copy.astype(jnp.float32) + partner.astype(jnp.float32))).astype(jnp.bfloat16)


def per_device(
    step_index,
    tokens,
    cotangent,
    w_query,
    w_key,
    w_value,
    w_out,
    last_query,
    last_key,
    last_value,
    last_out,
    query_gain,
    key_gain,
):
    head_dim = query_gain.shape[0]
    q_width = w_query.shape[2]
    k_width = w_key.shape[2]
    row_count = tokens.shape[0]
    levels = lax.axis_size("rep").bit_length() - 1
    normed, norm_back = jax.vjp(rms_rows, tokens.astype(jnp.float32))
    gathered = lax.all_gather(normed.astype(jnp.bfloat16), "tp", axis=0, tiled=True)
    length = gathered.shape[0]
    cosine_table, sine_table = rope_tables(length, head_dim)
    joined = jnp.concatenate([w_query[0], w_key[0], w_value[0]], axis=1)
    projected = jnp.dot(gathered, joined, preferred_element_type=jnp.float32)
    q_shaped, q_back = jax.vjp(
        lambda inner_raw: shape_heads(inner_raw, query_gain, cosine_table, sine_table),
        projected[:, :q_width],
    )
    k_shaped, k_back = jax.vjp(
        lambda inner_raw: shape_heads(inner_raw, key_gain, cosine_table, sine_table),
        projected[:, q_width : q_width + k_width],
    )
    query_rows = q_shaped.astype(jnp.bfloat16)
    key_rows = k_shaped.astype(jnp.bfloat16)
    value_rows = projected[:, q_width + k_width :].astype(jnp.bfloat16)
    attended = attend(query_rows, key_rows, value_rows, head_dim)
    out_weight = w_out[0]
    shard_rows = lax.all_gather(cotangent, "tp", axis=0, tiled=True)
    part_rows = lax.dot_general(
        shard_rows, out_weight, (((1,), (1,)), ((), ())), preferred_element_type=jnp.float32
    )
    grad_running = lax.dot_general(
        attended, shard_rows, (((0,), (0,)), ((), ())), preferred_element_type=jnp.float32
    )
    moved_out = advance(out_weight, last_out[0], grad_running)
    d_query, d_keys, d_values = attend_back(
        query_rows, key_rows, value_rows, part_rows.astype(jnp.bfloat16), head_dim
    )
    d_proj = jnp.concatenate(
        [
            q_back(d_query)[0].astype(jnp.bfloat16),
            k_back(d_keys)[0].astype(jnp.bfloat16),
            d_values.astype(jnp.bfloat16),
        ],
        axis=1,
    )
    grad_joined = lax.dot_general(
        gathered, d_proj, (((0,), (0,)), ((), ())), preferred_element_type=jnp.float32
    )
    summed = lax.psum(
        lax.dot_general(
            d_proj, joined, (((1,), (1,)), ((), ())), preferred_element_type=jnp.float32
        ).astype(jnp.bfloat16),
        "tp",
    ).astype(jnp.float32)
    own_rows = lax.dynamic_slice_in_dim(summed, lax.axis_index("tp") * row_count, row_count, 0)
    d_tokens = (norm_back(own_rows)[0] + cotangent.astype(jnp.float32)).astype(jnp.bfloat16)
    last_joined = jnp.concatenate([last_query[0], last_key[0], last_value[0]], axis=1)
    moved_joined = advance(joined, last_joined, grad_joined)

    def all_mover(exponent):

        def moving(values):
            return jax.tree.map(
                lambda part, own: part.astype(own.dtype),
                passed_along(shortened(values), "rep", 1 << exponent),
                values,
            )

        return moving

    flattened = jnp.concatenate([moved_joined.reshape(-1), moved_out.reshape(-1)])
    received = lax.switch(
        step_index[0] % levels, [all_mover(exponent) for exponent in range(levels)], flattened
    )
    partner_joined = received[: moved_joined.size].reshape(moved_joined.shape)
    partner_out = received[moved_joined.size :].reshape(moved_out.shape)
    new_joined = average(moved_joined, partner_joined)
    new_query = new_joined[:, :q_width][None]
    new_key = new_joined[:, q_width : q_width + k_width][None]
    new_value = new_joined[:, q_width + k_width :][None]
    new_out = average(moved_out, partner_out)[None]
    return (new_query, new_key, new_value, new_out, d_tokens)


def solution(mesh):
    placed = (
        P(),
        P(("rep", "tp"), None),
        P(("rep", "tp"), None),
        P("rep", None, "tp"),
        P("rep", None, "tp"),
        P("rep", None, "tp"),
        P("rep", "tp", None),
        P("rep", None, "tp"),
        P("rep", None, "tp"),
        P("rep", None, "tp"),
        P("rep", "tp", None),
        P(),
        P(),
    )
    return jax.shard_map(
        per_device,
        mesh=mesh,
        in_specs=placed,
        out_specs=(
            P("rep", None, "tp"),
            P("rep", None, "tp"),
            P("rep", None, "tp"),
            P("rep", "tp", None),
            P(("rep", "tp"), None),
        ),
        check_vma=False,
    )
```

profile of v0, /device:TPU:2, one launch (start us, length us, event | category | flops | bytes accessed | tf_op | source)
XLA Modules:
  0.0 423.0 jit_solution(15469774430719132838)
XLA Ops:
  8.5 2.0 fusion.55
  12.6 2.8 fusion.65
  15.4 74.4 %all-gather.3.cloned.1.call-done = bf16[1024,2048]{1,0:T(8,128)(2,1)} async-done(((bf16[128,2048]{1,0:T(8,128)(2,1)}), bf16[1024,2048]{1,0:T(8,128)(2,1)}) %all-gather.3.cloned.1.call-update) | async-done | bytes 4194320 | tf_op jit(solution)/shard_map/all_gather | solution.py:162
  89.8 5.1 %fusion.83 = f32[1024,512]{0,1:T(8,128)S(1)} fusion(bf16[1024,2048]{1,0:T(8,128)(2,1)} %all-gather.3.cloned.1.call-done, bf16[2048,128]{1,0:T(8,128)(2,1)S(1)} %bitcast.250, bf16[2048,128]{1,0:T(8,128)(2,1)} %bitcast.252, bf16[2048,256]{1,0:T(8,128)(2,1)} %bitcast.245), kind=kOutput, calls=%fused_computation.137 | convolution fusion | flops 2153775104 | bytes 8388608 | tf_op jit(solution)/shard_map/dot_general | solution.py:166
  96.4 70.4 %all-gather.5.cloned.1.call-done = bf16[1024,2048]{1,0:T(8,128)(2,1)} async-done(((bf16[128,2048]{1,0:T(8,128)(2,1)}), bf16[1024,2048]{1,0:T(8,128)(2,1)}) %all-gather.5.cloned.1.call-update) | async-done | bytes 4194320 | tf_op jit(solution)/shard_map/all_gather | solution.py:180
  166.8 3.6 convolution_convert_fusion.1
  173.5 1.7 subtract_convert_fusion.1
  178.9 1.6 fusion
  186.0 1.9 fusion.37
  189.4 1.6 fusion.4
  191.1 2.2 fusion.48
  195.6 1.6 fusion.16
  203.5 6.1 %convolution_convert_fusion = bf16[1024,2048]{1,0:T(8,128)(2,1)} fusion(bf16[1024,128]{0,1:T(8,128)(2,1)} %fusion.48, bf16[1024,128]{0,1:T(8,128)(2,1)S(1)} %fusion.70, bf16[1024,256]{0,1:T(8,128)(2,1)S(1)} %bitcast.239, bf16[2048,128]{1,0:T(8,128)(2,1)} %bitcast.249, bf16[2048,128]{1,0:T(8,128)(2,1)} %bitcast.253, bf16[2048,256]{1,0:T(8,128)(2,1)} %bitcast.246), kind=kOutput, calls=%fused_computation.18 | convolution fusion | flops 2159017984 | bytes 7340032 | tf_op jit(solution)/shard_map/dot_general | solution.py:203
  209.6 6.0 %subtract_convert_fusion = bf16[2048,512]{1,0:T(8,128)(2,1)S(1)} fusion(bf16[1024,2048]{1,0:T(8,128)(2,1)} %all-gather.3.cloned.1.call-done, bf16[2048,128]{1,0:T(8,128)(2,1)} %bitcast.255, bf16[2048,128]{1,0:T(8,128)(2,1)} %bitcast.256, bf16[2048,256]{1,0:T(8,128)(2,1)} %bitcast.248, bf16[1024,128]{0,1:T(8,128)(2,1)} %fusion.48, ...), kind=kOutput, calls=%fused_computation.15 | convolution fusion | flops 2168455168 | bytes 11534336 | tf_op jit(solution)/shard_map/dot_general | solution.py:199
  216.7 9.2 %pad_maximum_fusion = bf16[1572864]{0:T(1024)(128)(2,1)S(1)} fusion(bf16[524288]{0:T(1024)(128)(2,1)S(1)} %bitcast.238, bf16[1048576]{0:T(1024)(128)(2,1)S(1)} %bitcast.234), kind=kLoop, calls=%fused_computation.25 | loop fusion | flops 6291456 | bytes 6291456 | tf_op jit(solution)/shard_map/concatenate | solution.py:224
  226.0 69.9 %conditional.1 = (bf16[1572864]{0:T(1024)(128)(2,1)}) conditional(s32[]{:T(128)} %clamp.3, bf16[1572864]{0:T(1024)(128)(2,1)S(1)} %pad_maximum_fusion, bf16[1572864]{0:T(1024)(128)(2,1)S(1)} %pad_maximum_fusion, bf16[1572864]{0:T(1024)(128)(2,1)S(1)} %pad_maximum_fusion, ...), branch_computations={%region_11.12_spmd, %region_12.13_spmd, %region_13.14_spmd, %regio... | conditional | bytes 12582960 | solution.py:225
  227.7 68.1 %collective-permute-done.4 = bf16[1572864]{0:T(1024)(128)(2,1)} collective-permute-done((bf16[1572864]{0:T(1024)(128)(2,1)S(1)}, bf16[1572864]{0:T(1024)(128)(2,1)}, u32[]{:S(2)}, u32[]{:S(2)}) %collective-permute-start.4) | collective-permute-done | bytes 3145760 | tf_op jit(solution)/shard_map/cond/branch_4_fun/ppermute | solution.py:24
  295.8 3.8 slice_convert_fusion
  299.7 2.7 slice_convert_fusion.1
  302.4 1.7 reshape.344
  304.1 4.9 %reshape.343 = f32[2048,512]{1,0:T(8,128)} reshape(f32[1048576]{0:T(1024)} %slice_convert_fusion) | data formatting | bytes 8388608 | tf_op jit(solution)/shard_map/convert_element_type | solution.py:138
  309.0 4.0 multiply_convert_fusion
  316.4 96.3 %all-reduce.6.cloned.1.call-done = bf16[1024,2048]{1,0:T(8,128)(2,1)} async-done(((bf16[1024,2048]{1,0:T(8,128)(2,1)}), bf16[1024,2048]{1,0:T(8,128)(2,1)}) %all-reduce.6.cloned.1.call-update) | async-done | bytes 4194320 | tf_op jit(solution)/shard_map/psum | solution.py:202
  414.0 2.2 fusion.53
  (95 shorter events, 33.5 us)
Async XLA Ops:
  7.2 82.6 %copy-start.19 = (bf16[1,2048,128]{2,1,0:T(8,128)(2,1)S(1)}, bf16[1,2048,128]{2,1,0:T(8,128)(2,1)}, u32[]{:S(2)}) copy-start(bf16[1,2048,128]{2,1,0:T(8,128)(2,1)} %param.23) | copy-start | bytes 1572868
  7.2 82.6 %all-gather.3.cloned.1.call-start = ((), (), s32[]{:S(2)}) async-start(), calls=%async_computation | async-start | bytes 4718592 | tf_op jit(solution)/shard_map/all_gather | solution.py:162
  10.5 156.3 %all-gather.5.cloned.1.call-start = ((), (), s32[]{:S(2)}) async-start(), calls=%async_computation.1 | async-start | bytes 4718592 | tf_op jit(solution)/shard_map/all_gather | solution.py:180
  11.3 401.4 %all-reduce.6.cloned.1.call-start = ((), (), s32[]{:S(2)}) async-start(), calls=%async_computation.2 | async-start | bytes 8388608 | tf_op jit(solution)/shard_map/psum | solution.py:202
  89.8 77.0 %copy-start.16 = (bf16[1,256,2048]{2,1,0:T(8,128)(2,1)S(1)}, bf16[1,256,2048]{2,1,0:T(8,128)(2,1)}, u32[]{:S(2)}) copy-start(bf16[1,256,2048]{2,1,0:T(8,128)(2,1)} %param.24) | copy-start | bytes 3145732
  96.3 74.9 %copy-start.12 = (f32[128]{0:T(128)S(1)}, f32[128]{0:T(128)}, u32[]{:S(2)}) copy-start(f32[128]{0:T(128)} %param.30) | copy-start | bytes 1540
  96.4 76.4 %slice-start = ((f32[1024,512]{0,1:T(8,128)}), f32[1024,256]{0,1:T(8,128)S(1)}, s32[]{:S(2)}) async-start(f32[1024,512]{0,1:T(8,128)} %copy-done), calls=%async_computation.3 | async-start | bytes 2097152 | tf_op jit(solution)/shard_map/slice | solution.py:169
  166.8 4.5 %copy-start.1 = (f32[1024,512]{0,1:T(8,128)S(1)}, f32[1024,512]{0,1:T(8,128)}, u32[]{:S(2)}) copy-start(f32[1024,512]{0,1:T(8,128)} %copy-done) | copy-start | bytes 6291460
  170.4 2.7 copy-start.13
  175.3 2.1 copy-start.2
  186.0 1.9 copy-start.11
  191.0 2.3 copy-start.14
  191.1 2.5 copy-start.15
  191.1 2.9 copy-start.17
  195.4 1.8 copy-start.7
  198.2 2.6 copy-start.5
  198.2 2.6 copy-start.6
  203.5 6.1 %copy-start.18 = (bf16[1,2048,256]{2,1,0:T(8,128)(2,1)S(1)}, bf16[1,2048,256]{2,1,0:T(8,128)(2,1)}, u32[]{:S(2)}) copy-start(bf16[1,2048,256]{2,1,0:T(8,128)(2,1)} %param.21) | copy-start | bytes 3145732
  203.5 6.1 %copy-start.20 = (bf16[1,2048,128]{2,1,0:T(8,128)(2,1)S(1)}, bf16[1,2048,128]{2,1,0:T(8,128)(2,1)}, u32[]{:S(2)}) copy-start(bf16[1,2048,128]{2,1,0:T(8,128)(2,1)} %param.23) | copy-start | bytes 1572868
  215.6 10.3 %copy-start.3 = (bf16[2048,512]{1,0:T(8,128)(2,1)}, bf16[2048,512]{1,0:T(8,128)(2,1)S(1)}, u32[]{:S(2)}) copy-start(bf16[2048,512]{1,0:T(8,128)(2,1)S(1)} %subtract_convert_fusion) | copy-start | bytes 6291460
  226.2 69.6 %collective-permute-start.4 = (bf16[1572864]{0:T(1024)(128)(2,1)S(1)}, bf16[1572864]{0:T(1024)(128)(2,1)}, u32[]{:S(2)}, u32[]{:S(2)}) collective-permute-start(bf16[1572864]{0:T(1024)(128)(2,1)S(1)} %param.4), channel_id=1, source_target_pairs={{0,128},{8,136},{16,144},{24,152},{32,160},{40,168},{48,176},{56,1... | collective-permute-start | bytes 9437192 | tf_op jit(solution)/shard_map/cond/branch_4_fun/ppermute | solution.py:24
  313.0 2.1 copy-start.8
  313.0 99.7 %copy-start.4 = (bf16[128,2048]{1,0:T(8,128)(2,1)S(1)}, bf16[128,2048]{1,0:T(8,128)(2,1)}, u32[]{:S(2)}) copy-start(bf16[128,2048]{1,0:T(8,128)(2,1)} %param.19) | copy-start | bytes 1572868
  314.0 100.0 %copy-start.9 = (bf16[128,2048]{1,0:T(8,128)(2,1)S(1)}, bf16[128,2048]{1,0:T(8,128)(2,1)}, u32[]{:S(2)}) copy-start(bf16[128,2048]{1,0:T(8,128)(2,1)} %param.20) | copy-start | bytes 1572868
  (2 other events, 2.9 us)
Sparse Core Ops, SparseCore 0:
  11.2 78.4 all-gather.2
  92.4 74.3 all-gather.4
  299.8 112.8 all-reduce.5
where the time goes:
time: 430 us; the launch traced here: 423 us
  waiting for transfers between devices  310 us (72%)
  other arithmetic  44 us (10%)
  matrix products  38.5 us (9%)
  between operations  15.2 us (4%)
  local copies, waits for them, and re-layouts  13.4 us (3%)
    psum x1, waiting for transfers between devices, per_device(): lax.psum(lax.dot_general(d_proj, joined, (((1,), (1,)), ((), ())), prefer...  96.3 us
    all_gather x1, waiting for transfers between devices, per_device(): lax.all_gather(normed.astype(jnp.bfloat16), 'tp', axis=0, tiled=True)  74.4 us
    all_gather x1, waiting for transfers between devices, per_device(): shard_rows = lax.all_gather(cotangent, 'tp', axis=0, tiled=True)  70.4 us
    ppermute x1, waiting for transfers between devices, passed_along(): lax.ppermute(array, axis, [(i, (i + by) % peers) for i in range(peers)])  68.1 us
    dot_general x12, matrix products, product(): jnp.einsum(pattern, left_in, right_in, preferred_element_type=jnp.float32)  16.3 us
    concatenate x1, other arithmetic, per_device(): jnp.concatenate([moved_joined.reshape(-1), moved_out.reshape(-1)])  9.23 us
  transfers between devices with their start and end apart: 4, of which 4 were waited for; matrix products, arithmetic and copies ran while one was open for 6% of the time, Pallas kernels for 0%

commit v1 on v0

v1 whole, which is shorter than its diff:
```python
import functools
import math

import jax
import jax.numpy as jnp
import numpy as np
from jax import lax
from jax.experimental import pallas as pl
from jax.experimental.pallas import tpu as pltpu
from jax.sharding import PartitionSpec as P

EPSILON = 1e-06
MOMENTUM = 0.9
LEARNING_RATE = 0.001
MASKED = -1e30
MESH = pl.DeviceIdType.MESH
BF16 = jnp.bfloat16
F32 = jnp.float32
HD = 128
SCALE = HD ** (-0.5)
LOG2E = math.log2(math.e)
QB = 256
ROWS, COLS, LEN, QKV, QW = 128, 2048, 1024, 512, 256
X_ROWS = 512

YM, YP, X0, Y2A, Y2B, XM, XP, X2A, X2B = range(9)


def dot(a, b):
    return jnp.dot(a, b, preferred_element_type=F32)


def dot_t(a, b):
    return lax.dot_general(a, b, (((1,), (1,)), ((), ())), preferred_element_type=F32)


def rope_tables(length):
    half = HD // 2
    inverse = np.exp(np.arange(half, dtype=np.float32) * np.float32(-2.0 * math.log(1000000.0) / HD))
    angles = np.arange(length, dtype=np.float32)[:, None] * inverse[None, :].astype(np.float32)
    cosine, sine = np.cos(angles), np.sin(angles)
    return (
        np.concatenate([cosine, cosine], axis=1).astype(np.float32),
        np.concatenate([-sine, sine], axis=1).astype(np.float32),
    )


def kernel(
    shift,
    tokens, cotangent, w_query, w_key, w_value, w_out, l_query, l_key, l_value, l_out,
    query_gain, key_gain, cosine, sine,
    o_query, o_key, o_value, o_out, o_tokens,
    tok, cot_own, normed, cots, normed_t, w_all, l_all, wo, lo, cos_t, sin_t,
    raw, q_rows, k_rows, v_rows, prob, attended, d_att, d_keys, d_values, d_proj,
    arrived, moved, moved_out, partner, partner_out,
    load_sem, store_sem, ag_send, ag_recv, rs_send, rs_recv, ex_send, ex_recv,
):
    reps = lax.axis_size("rep")
    rep = lax.axis_index("rep")
    tp = lax.axis_index("tp")
    h, y = tp // 4, tp % 4
    hx, yp, ym, y2 = 1 - h, (y + 1) % 4, (y + 3) % 4, (y + 2) % 4
    ahead, behind = (rep + shift) % reps, (rep + reps - shift) % reps

    def rows_of(hh, yy):
        return pl.ds(pl.multiple_of((hh * 4 + yy) * ROWS, ROWS), ROWS)

    def half_of(hh, yy, second):
        return pl.ds(pl.multiple_of((hh * 4 + yy) * ROWS + second * (ROWS // 2), ROWS // 2), ROWS // 2)

    own = rows_of(h, y)

    loads = {}

    def load(name, src, dst):
        loads[name] = pltpu.make_async_copy(src, dst, load_sem.at[len(loads)])
        loads[name].start()

    load("tok", tokens, tok)
    load("cot", cotangent, cots.at[own])
    load("cot2", cotangent, cot_own)
    load("wq", w_query, w_all.at[:, 0:256])
    load("wk", w_key, w_all.at[:, 256:384])
    load("wv", w_value, w_all.at[:, 384:512])
    load("cos", cosine, cos_t)
    load("sin", sine, sin_t)
    load("wo", w_out, wo)
    load("lo", l_out, lo)
    load("lq", l_query, l_all.at[:, 0:256])
    load("lk", l_key, l_all.at[:, 256:384])
    load("lv", l_value, l_all.at[:, 384:512])

    barrier = pltpu.get_barrier_semaphore()
    for step in range(1, 8):
        pl.semaphore_signal(barrier, inc=1, device_id={"tp": (tp + step) % 8}, device_id_type=MESH)
    pl.semaphore_signal(barrier, inc=1, device_id={"rep": ahead}, device_id_type=MESH)
    pl.semaphore_signal(barrier, inc=1, device_id={"rep": behind}, device_id_type=MESH)

    loads["tok"].wait()
    x = tok[...].astype(F32)
    normed[own, :] = (x * lax.rsqrt(jnp.mean(x * x, axis=-1, keepdims=True) + EPSILON)).astype(BF16)
    pl.semaphore_wait(barrier, 9)

    copies = {}

    def gather(which, tag, rows, target):
        buf = (normed, cots)[which]
        copies[which, tag] = pltpu.make_async_remote_copy(
            src_ref=buf.at[rows],
            dst_ref=buf.at[rows],
            send_sem=ag_send.at[which, tag],
            recv_sem=ag_recv.at[which, tag],
            device_id={"tp": target},
            device_id_type=MESH,
        )
        copies[which, tag].start()

    def got(which, *tags):
        for tag in tags:
            copies[which, tag].wait_recv()

    t_yp, t_ym, t_x = h * 4 + yp, h * 4 + ym, hx * 4 + y

    def first(which):
        gather(which, YM, own, t_yp)
        gather(which, YP, own, t_ym)
        gather(which, X0, own, t_x)

    def second(which):
        got(which, YM)
        gather(which, Y2A, half_of(h, ym, 0), t_yp)
        got(which, YP)
        gather(which, Y2B, half_of(h, yp, 1), t_ym)
        got(which, X0)
        gather(which, XM, rows_of(hx, y), t_yp)
        gather(which, XP, rows_of(hx, y), t_ym)

    def third(which):
        got(which, Y2A)
        gather(which, X2A, half_of(h, y2, 0), t_x)
        got(which, Y2B)
        gather(which, X2B, half_of(h, y2, 1), t_x)

    def normed_rows(values):
        return values * lax.rsqrt(jnp.mean(values * values, axis=-1, keepdims=True) + EPSILON)

    def turned(values, rows):
        return values * cos_t[rows, :] + pltpu.roll(values, HD // 2, 1) * sin_t[rows, :]

    def project(hh, yy):
        rows = rows_of(hh, yy)
        block = normed[rows, :]
        out = dot(block, w_all[...])
        raw[rows, :] = out[:, :384]
        for head in range(2):
            q_rows[head, rows, :] = turned(
                normed_rows(out[:, head * HD : (head + 1) * HD]) * query_gain[...], rows
            ).astype(BF16)
        k_rows[rows, :] = turned(normed_rows(out[:, 256:384]) * key_gain[...], rows).astype(BF16)
        v_rows[rows, :] = out[:, 384:].astype(BF16)
        normed_t[:, rows] = block.T

    def project_some(pairs):
        for pair in pairs:
            project(*pair)

    def forward(at):
        width = (at + 1) * QB

        def one(head, carry):
            rows = pl.ds(at * QB, QB)
            scores = dot_t(q_rows[head, rows, :], k_rows[0:width, :]) * (SCALE * LOG2E)
            row_pos = at * QB + lax.broadcasted_iota(jnp.int32, (QB, width), 0)
            col_pos = lax.broadcasted_iota(jnp.int32, (QB, width), 1)
            scores = jnp.where(col_pos <= row_pos, scores, MASKED)
            raised = jnp.exp2(scores - jnp.max(scores, axis=-1, keepdims=True))
            p = raised * (1.0 / jnp.sum(raised, axis=-1, keepdims=True))
            prob[head, rows, 0:width] = p
            attended[head, rows, :] = dot(p.astype(BF16), v_rows[0:width, :]).astype(BF16)
            return carry

        lax.fori_loop(0, 2, one, 0)

    def backward(at):
        width = (at + 1) * QB

        for head in range(2):
            rows = pl.ds(at * QB, QB)
            p = prob[head, rows, 0:width]
            up = d_att[head, rows, :]
            d_prob = dot_t(up, v_rows[0:width, :])
            centred = d_prob - jnp.sum(p * d_prob, axis=-1, keepdims=True)
            d_scores = (p * centred * SCALE).astype(BF16)
            d_values[0:width, :] += dot(p.astype(BF16).T, up)
            d_keys[0:width, :] += dot(d_scores.T, q_rows[head, rows, :])
            d_query = dot(d_scores, k_rows[0:width, :])
            d_proj[rows, head * HD : (head + 1) * HD] = unshaped(
                d_query, raw[rows, head * HD : (head + 1) * HD], query_gain, rows
            )

    def unshaped(d_turned, before, gain, rows):
        d_grouped = d_turned * cos_t[rows, :] + pltpu.roll(d_turned * sin_t[rows, :], HD // 2, 1)
        d_norm = d_grouped * gain[...]
        inverse = lax.rsqrt(jnp.mean(before * before, axis=-1, keepdims=True) + EPSILON)
        inner = jnp.mean(before * d_norm, axis=-1, keepdims=True)
        return (inverse * d_norm - before * (inverse * inverse * inverse * inner)).astype(BF16)

    def upstream(hh, yy):
        rows = rows_of(hh, yy)
        out = dot_t(cots[rows, :], wo[...]).astype(BF16)
        d_att[0, rows, :] = out[:, :HD]
        d_att[1, rows, :] = out[:, HD:]

    first(0)
    for name in ("wq", "wk", "wv", "cos", "sin", "cot"):
        loads[name].wait()
    project(h, y)
    second(0)
    project_some([(h, ym), (h, yp), (hx, y)])
    third(0)
    first(1)
    project(h, y2)
    got(0, XM, XP)
    project_some([(hx, ym), (hx, yp)])
    got(0, X2A, X2B)
    project(hx, y2)
    second(1)
    forward(0)
    forward(1)
    third(1)
    loads["wo"].wait()
    loads["lo"].wait()
    forward(2)
    forward(3)
    upstream(h, y)
    upstream(h, ym)
    upstream(h, yp)
    upstream(hx, y)
    upstream(h, y2)
    got(1, XM, XP)
    upstream(hx, ym)
    upstream(hx, yp)
    got(1, X2A, X2B)
    upstream(hx, y2)

    exchange = []

    def send_on(src, dst):
        at = len(exchange)
        copy = pltpu.make_async_remote_copy(
            src_ref=src,
            dst_ref=dst,
            send_sem=ex_send.at[at],
            recv_sem=ex_recv.at[at],
            device_id={"rep": ahead},
            device_id_type=MESH,
        )
        copy.start()
        exchange.append(copy)

    for head in range(2):
        rows = pl.ds(head * HD, HD)
        att_t = attended[head].T

        def out_step(at, carry):
            cols = pl.ds(pl.multiple_of(at * 512, 512), 512)
            grad = dot(att_t, cots[:, cols])
            moved_out[rows, cols] = (
                wo[rows, cols].astype(F32)
                + MOMENTUM * lo[rows, cols].astype(F32)
                - LEARNING_RATE * grad
            ).astype(BF16)
            return carry

        lax.fori_loop(0, 4, out_step, 0)
        send_on(moved_out.at[rows], partner_out.at[rows])

    d_keys[...] = jnp.zeros_like(d_keys)
    d_values[...] = jnp.zeros_like(d_values)
    for at in range(LEN // QB):
        backward(at)

    def key_step(at, carry):
        rows = pl.ds(pl.multiple_of(at * 256, 256), 256)
        d_proj[rows, 256:384] = unshaped(d_keys[rows, :], raw[rows, 256:384], key_gain, rows)
        d_proj[rows, 384:512] = d_values[rows, :].astype(BF16)
        return carry

    lax.fori_loop(0, 4, key_step, 0)

    for copy in copies.values():
        copy.wait_send()

    terms = cots

    def term_step(at, carry):
        rows = pl.ds(pl.multiple_of(at * 256, 256), 256)
        terms[rows, :] = dot_t(d_proj[rows, :], w_all[...]).astype(BF16)
        return carry

    lax.fori_loop(0, 4, term_step, 0)
    scatter = []
    for step in range(1, 8):
        target = (tp + step) % 8
        copy = pltpu.make_async_remote_copy(
            src_ref=terms.at[pl.ds(pl.multiple_of(target * ROWS, ROWS), ROWS)],
            dst_ref=arrived.at[step - 1],
            send_sem=rs_send.at[step - 1],
            recv_sem=rs_recv.at[step - 1],
            device_id={"tp": target},
            device_id_type=MESH,
        )
        copy.start()
        scatter.append(copy)

    for name in ("lq", "lk", "lv"):
        loads[name].wait()
    for at in range(COLS // X_ROWS):

        def weight_step(sub, carry):
            rows = pl.ds(pl.multiple_of(at * X_ROWS + sub * 256, 256), 256)
            grad = dot(normed_t[rows, :], d_proj[...])
            moved[rows, :] = (
                w_all[rows, :].astype(F32)
                + MOMENTUM * l_all[rows, :].astype(F32)
                - LEARNING_RATE * grad
            ).astype(BF16)
            return carry

        lax.fori_loop(0, X_ROWS // 256, weight_step, 0)
        rows = pl.ds(at * X_ROWS, X_ROWS)
        send_on(moved.at[rows], partner.at[rows])

    for copy in scatter:
        copy.wait_recv()
    loads["cot2"].wait()

    def token_step(at, carry):
        rows = pl.ds(pl.multiple_of(at * 32, 32), 32)
        total = terms[pl.ds(pl.multiple_of(tp * ROWS + at * 32, 32), 32), :].astype(F32)
        for step in range(7):
            total = total + arrived[step, rows, :].astype(F32)
        x = tok[rows, :].astype(F32)
        inverse = lax.rsqrt(jnp.mean(x * x, axis=-1, keepdims=True) + EPSILON)
        inner = jnp.mean(x * total, axis=-1, keepdims=True)
        tok[rows, :] = (
            inverse * total
            - x * (inverse * inverse * inverse * inner)
            + cot_own[rows, :].astype(F32)
        ).astype(BF16)
        return carry

    lax.fori_loop(0, ROWS // 32, token_step, 0)
    stores = []

    def store(src, dst):
        copy = pltpu.make_async_copy(src, dst, store_sem.at[len(stores)])
        copy.start()
        stores.append(copy)

    store(tok, o_tokens)

    def averaged(mine, theirs, rows):
        theirs[rows, :] = (0.5 * (mine[rows, :].astype(F32) + theirs[rows, :].astype(F32))).astype(BF16)

    for head in range(2):
        exchange[head].wait_recv()
        rows = pl.ds(head * HD, HD)
        averaged(moved_out, partner_out, rows)
        store(partner_out.at[rows], o_out.at[rows])
    for at in range(COLS // X_ROWS):
        exchange[2 + at].wait_recv()
        rows = pl.ds(at * X_ROWS, X_ROWS)
        averaged(moved, partner, rows)
        store(partner.at[rows, 0:256], o_query.at[rows])
        store(partner.at[rows, 256:384], o_key.at[rows])
        store(partner.at[rows, 384:512], o_value.at[rows])
    for copy in scatter:
        copy.wait_send()
    for copy in exchange:
        copy.wait_send()
    for copy in stores:
        copy.wait()


def training_step(exponent, arrays):
    def vmem(*shape, dtype=BF16):
        return pltpu.VMEM(shape, dtype)

    dma = pltpu.SemaphoreType.DMA
    any_spec = pl.BlockSpec(memory_space=pl.ANY)
    vmem_spec = pl.BlockSpec(memory_space=pltpu.VMEM)
    return pl.pallas_call(
        functools.partial(kernel, 1 << exponent),
        out_shape=(
            jax.ShapeDtypeStruct((COLS, 256), BF16),
            jax.ShapeDtypeStruct((COLS, 128), BF16),
            jax.ShapeDtypeStruct((COLS, 128), BF16),
            jax.ShapeDtypeStruct((256, COLS), BF16),
            jax.ShapeDtypeStruct((ROWS, COLS), BF16),
        ),
        in_specs=[any_spec] * 10 + [vmem_spec] * 2 + [any_spec] * 2,
        out_specs=(any_spec,) * 5,
        scratch_shapes=[
            vmem(ROWS, COLS),
            vmem(ROWS, COLS),
            vmem(LEN, COLS),
            vmem(LEN, COLS),
            vmem(COLS, LEN),
            vmem(COLS, QKV),
            vmem(COLS, QKV),
            vmem(QW, COLS),
            vmem(QW, COLS),
            vmem(LEN, HD, dtype=F32),
            vmem(LEN, HD, dtype=F32),
            vmem(LEN, 384, dtype=F32),
            vmem(2, LEN, HD),
            vmem(LEN, HD),
            vmem(LEN, HD),
            vmem(2, LEN, LEN, dtype=F32),
            vmem(2, LEN, HD),
            vmem(2, LEN, HD),
            vmem(LEN, HD, dtype=F32),
            vmem(LEN, HD, dtype=F32),
            vmem(LEN, QKV),
            vmem(7, ROWS, COLS),
            vmem(COLS, QKV),
            vmem(QW, COLS),
            vmem(COLS, QKV),
            vmem(QW, COLS),
            dma((13,)),
            dma((3 + 3 * (COLS // X_ROWS),)),
            dma((2, 9)),
            dma((2, 9)),
            dma((7,)),
            dma((7,)),
            dma((2 + COLS // X_ROWS,)),
            dma((2 + COLS // X_ROWS,)),
        ],
        compiler_params=pltpu.CompilerParams(
            collective_id=exponent, has_side_effects=True, vmem_limit_bytes=60 << 20
        ),
        cost_estimate=pl.CostEstimate(
            flops=11_000_000_000, bytes_accessed=12_000_000, transcendentals=2_000_000
        ),
    )(*arrays)


def per_device(
    step_index, tokens, cotangent, w_query, w_key, w_value, w_out,
    last_query, last_key, last_value, last_out, query_gain, key_gain,
):
    levels = lax.axis_size("rep").bit_length() - 1
    cosine, sine = rope_tables(LEN)
    arrays = (
        tokens, cotangent, w_query[0], w_key[0], w_value[0], w_out[0],
        last_query[0], last_key[0], last_value[0], last_out[0],
        query_gain[None], key_gain[None], jnp.asarray(cosine), jnp.asarray(sine),
    )
    new_query, new_key, new_value, new_out, d_tokens = lax.switch(
        step_index[0] % levels,
        [functools.partial(training_step, exponent) for exponent in range(levels)],
        arrays,
    )
    return (new_query[None], new_key[None], new_value[None], new_out[None], d_tokens)


def solution(mesh):
    placed = (
        P(),
        P(("rep", "tp"), None),
        P(("rep", "tp"), None),
        P("rep", None, "tp"),
        P("rep", None, "tp"),
        P("rep", None, "tp"),
        P("rep", "tp", None),
        P("rep", None, "tp"),
        P("rep", None, "tp"),
        P("rep", None, "tp"),
        P("rep", "tp", None),
        P(),
        P(),
    )
    return jax.shard_map(
        per_device,
        mesh=mesh,
        in_specs=placed,
        out_specs=(
            P("rep", None, "tp"),
            P("rep", None, "tp"),
            P("rep", None, "tp"),
            P("rep", "tp", None),
            P(("rep", "tp"), None),
        ),
        check_vma=False,
    )
```

time: 430 us -> 234 us (0.54)
  waiting for transfers between devices: 310 us -> 0 us
  Pallas kernels: 0 us -> 210 us
  other arithmetic: 44 us -> 0 us
  matrix products: 38.5 us -> 0 us
  loops' own time: 0.24 us -> 14.1 us
  between operations: 15.2 us -> 1.88 us
  local copies, waits for them, and re-layouts: 13.4 us -> 4.98 us
    pallas_call x0 -> x1, Pallas kernels: none -> 210 us  [training_step(): pl.pallas_call(functools.partial(kernel, 1 << exponent), out_shape=(jax.S...]
    all_gather x2 -> x0, waiting for transfers between devices: 145 us -> none  [the longest x1 74.4 us: per_device(): lax.all_gather(normed.astype(jnp.bfloat16), 'tp', axis=0, tiled=True)]
    psum x1 -> x0, waiting for transfers between devices: 96.3 us -> none  [per_device(): lax.psum(lax.dot_general(d_proj, joined, (((1,), (1,)), ((), ())), prefer...]
    ppermute x1 -> x0, waiting for transfers between devices: 68.1 us -> none  [passed_along(): lax.ppermute(array, axis, [(i, (i + by) % peers) for i in range(peers)])]
    dot_general x17 -> x0, matrix products: 38.5 us -> none  [the longest x12 16.3 us: product(): jnp.einsum(pattern, left_in, right_in, preferred_element_type=jnp.float32)]
    convert_element_type x7 -> x0, other arithmetic: 16 us -> none  [the longest x2 6.51 us: average(): partner.astype(jnp.float32)]
    another operation x1, loops' own time: 0.24 us -> 14.1 us  [per_device(): lax.switch(step_index[0] % levels, [functools.partial(training_step, expo...]
    concatenate x3 -> x0, other arithmetic: 10.7 us -> none  [the longest x1 9.23 us: per_device(): jnp.concatenate([moved_joined.reshape(-1), moved_out.reshape(-1)])]
  transfers between devices with their start and end apart: 4 -> 0, of which waited for: 4 -> 0; matrix products, arithmetic and copies ran while one was open for 6% -> 0% of each run, Pallas kernels for 0% -> 0%
where the time goes in v1:
time: 234 us; the launch traced here: 231 us
  Pallas kernels  210 us (90%)
  loops' own time  14.1 us (6%)
  local copies, waits for them, and re-layouts  4.98 us (2%)
    pallas_call x1, Pallas kernels, training_step(): pl.pallas_call(functools.partial(kernel, 1 << exponent), out_shape=(jax.S...  210 us
    another operation x1, loops' own time, per_device(): lax.switch(step_index[0] % levels, [functools.partial(training_step, expo...  14.1 us
    unnamed x9, local copies, waits for them, and re-layouts  4.98 us

profile of v1, /device:TPU:2, one launch (start us, length us, event | category | flops | bytes accessed | tf_op | source)
XLA Modules:
  0.0 230.7 jit_solution(16462263791355890628)
XLA Ops:
  1.3 0.0 copy-start
  1.3 0.0 copy-start.1
  1.3 0.6 copy-done
  1.9 0.0 copy-done.1
  2.0 223.8 %conditional.1 = ((bf16[2048,256]{1,0:T(8,128)(2,1)S(1)}, bf16[2048,128]{1,0:T(8,128)(2,1)S(1)}, bf16[2048,128]{1,0:T(8,128)(2,1)S(1)}, bf16[256,2048]{1,0:T(8,128)(2,1)S(1)}, bf16[128,2048]{1,0:T(8,128)(2,1)S(1)})) conditional(s32[]{:T(128)} %clamp.3, (bf16[128,2048]{1,0:T(8,128)(2,1)}, bf16[128,2048]{1,0:T(8,128)(2,1)}, ...), branch_computations={%region_0.1_spmd, %region_1.2_spmd, %region_2.3_spmd, %region_3.4_... | conditional | flops 11000000512 | bytes 12000008 | solution.py:460
  6.1 209.8 %branch_3_fun.1 = (bf16[2048,256]{1,0:T(8,128)(2,1)S(1)}, bf16[2048,128]{1,0:T(8,128)(2,1)S(1)}, bf16[2048,128]{1,0:T(8,128)(2,1)S(1)}, bf16[256,2048]{1,0:T(8,128)(2,1)S(1)}, bf16[128,2048]{1,0:T(8,128)(2,1)S(1)}) custom-call(bf16[128,2048]{1,0:T(8,128)(2,1)} %get-tuple-element.217.tokens, bf16[128,2048]{1,0:T(8,128)(2,1)} %get-tuple-element.218.cotangent, ...), custom_call_target="tpu_custom_call" | custom-call | flops 11000000512 | bytes 12000000 | tf_op jit(solution)/shard_map/cond/branch_3_fun/pallas_call | solution.py:393
  225.8 1.0 copy.51
  226.8 0.8 copy.52
  227.6 0.8 copy.53
  228.4 1.0 copy.54
  229.3 0.8 copy.55
Async XLA Ops:
  1.3 0.7 copy-start
  1.3 0.7 copy-start.1

commit v2 on v1

v2 whole, which is shorter than its diff:
```python
import functools
import math

import jax
import jax.numpy as jnp
import numpy as np
from jax import lax
from jax.experimental import pallas as pl
from jax.experimental.pallas import tpu as pltpu
from jax.sharding import PartitionSpec as P

EPSILON = 1e-06
MOMENTUM = 0.9
LEARNING_RATE = 0.001
MASKED = -1e30
MESH = pl.DeviceIdType.MESH
BF16 = jnp.bfloat16
F32 = jnp.float32
HD = 128
SCALE = HD ** (-0.5)
LOG2E = math.log2(math.e)
QB = 256
ROWS, COLS, LEN, QKV, QW = 128, 2048, 1024, 512, 256

YM, YP, X0, Y2A, Y2B, XM, XP, X2A, X2B = range(9)
RC, RP, RM, HA, HB, NX, NMA, NMB, NPA, NPB = range(10)


def dot(a, b):
    return jnp.dot(a, b, preferred_element_type=F32)


def dot_t(a, b):
    return lax.dot_general(a, b, (((1,), (1,)), ((), ())), preferred_element_type=F32)


def rope_tables(length):
    half = HD // 2
    inverse = np.exp(np.arange(half, dtype=np.float32) * np.float32(-2.0 * math.log(1000000.0) / HD))
    angles = np.arange(length, dtype=np.float32)[:, None] * inverse[None, :].astype(np.float32)
    cosine, sine = np.cos(angles), np.sin(angles)
    return (
        np.concatenate([cosine, cosine], axis=1).astype(np.float32),
        np.concatenate([-sine, sine], axis=1).astype(np.float32),
    )


def kernel(
    shift,
    tokens, cotangent, w_query, w_key, w_value, w_out, l_query, l_key, l_value, l_out,
    query_gain, key_gain, cosine, sine,
    o_query, o_key, o_value, o_out, o_tokens,
    tok, cot_own, normed, cots, normed_t, w_all, l_all, wo, lo, cos_t, sin_t,
    raw, q_rows, k_rows, v_rows, prob, att_t, d_att, d_keys, d_values, d_proj,
    arrived, moved, moved_out, partner, partner_out, relay,
    load_sem, store_sem, ag_send, ag_recv, rs_send, rs_recv, ex_send, ex_recv, relay_send, relay_recv,
):
    reps = lax.axis_size("rep")
    rep = lax.axis_index("rep")
    tp = lax.axis_index("tp")
    h, y = tp // 4, tp % 4
    hx, yp, ym, y2 = 1 - h, (y + 1) % 4, (y + 3) % 4, (y + 2) % 4
    ahead, behind = (rep + shift) % reps, (rep + reps - shift) % reps
    relayed = shift == 4
    ring = 16

    def along(start, by):
        return start // ring * ring + (start % ring + ring + by) % ring

    via = along(rep, -6)
    via_ahead = (along(rep, 6) + shift) % reps
    via_behind = along(behind, -6)

    def rows_of(hh, yy):
        return pl.ds(pl.multiple_of((hh * 4 + yy) * ROWS, ROWS), ROWS)

    def half_of(hh, yy, second):
        return pl.ds(pl.multiple_of((hh * 4 + yy) * ROWS + second * (ROWS // 2), ROWS // 2), ROWS // 2)

    own = rows_of(h, y)

    loads = {}

    def load(name, src, dst):
        loads[name] = pltpu.make_async_copy(src, dst, load_sem.at[len(loads)])
        loads[name].start()

    load("tok", tokens, tok)
    load("cot", cotangent, cots.at[own])
    load("cot2", cotangent, cot_own)
    load("wq", w_query, w_all.at[:, 0:256])
    load("wk", w_key, w_all.at[:, 256:384])
    load("wv", w_value, w_all.at[:, 384:512])
    load("cos", cosine, cos_t)
    load("sin", sine, sin_t)
    load("wo", w_out, wo)
    load("lo", l_out, lo)
    load("lq", l_query, l_all.at[:, 0:256])
    load("lk", l_key, l_all.at[:, 256:384])
    load("lv", l_value, l_all.at[:, 384:512])

    barrier = pltpu.get_barrier_semaphore()
    for step in range(1, 8):
        pl.semaphore_signal(barrier, inc=1, device_id={"tp": (tp + step) % 8}, device_id_type=MESH)
    partners = [ahead, behind]
    if relayed:
        partners += [via, along(rep, 6), via_ahead, via_behind]
    for device in partners:
        pl.semaphore_signal(barrier, inc=1, device_id={"rep": device}, device_id_type=MESH)

    loads["tok"].wait()
    x = tok[...].astype(F32)
    normed[own, :] = (x * lax.rsqrt(jnp.mean(x * x, axis=-1, keepdims=True) + EPSILON)).astype(BF16)
    pl.semaphore_wait(barrier, 7 + len(partners))

    t_yp, t_ym, t_x = h * 4 + yp, h * 4 + ym, hx * 4 + y
    own_half = (half_of(h, ym, 0), half_of(h, yp, 1))
    far_half = (half_of(h, y2, 0), half_of(h, y2, 1))
    plans = {
        YM: (own, t_yp),
        YP: (own, t_ym),
        X0: (own, t_x),
        Y2A: (own_half[0], t_yp),
        Y2B: (own_half[1], t_ym),
        XM: (rows_of(hx, y), t_yp),
        XP: (rows_of(hx, y), t_ym),
        X2A: (far_half[0], t_x),
        X2B: (far_half[1], t_x),
    }

    def gather(which, tag):
        rows, target = plans[tag]
        buf = (normed, cots)[which]
        return pltpu.make_async_remote_copy(
            src_ref=buf.at[rows],
            dst_ref=buf.at[rows],
            send_sem=ag_send.at[which, tag],
            recv_sem=ag_recv.at[which, tag],
            device_id={"tp": target},
            device_id_type=MESH,
        )

    def start(which, *tags):
        for tag in tags:
            gather(which, tag).start()

    def got(which, *tags):
        for tag in tags:
            gather(which, tag).wait_recv()

    def first(which):
        start(which, YM, YP, X0)

    def second(which):
        got(which, YM)
        start(which, Y2A)
        got(which, YP)
        start(which, Y2B)
        got(which, X0)
        start(which, XM, XP)

    def third(which):
        got(which, Y2A)
        start(which, X2A)
        got(which, Y2B)
        start(which, X2B)

    order = tuple(zip((0, 0, 0, 1, 0, 1, 1, 1), (0, 3, 1, 0, 2, 3, 1, 2)))

    def over_blocks(offsets, before, work, after=None):
        def body(i, carry):
            far, turn = carry
            for step, action in before.items():
                pl.when(i == step)(action)
            hh = (h + far % 2) % 2
            work(rows_of(hh, (y + turn % 4) % 4))
            for step, action in (after or {}).items():
                pl.when(i == step)(action)
            return far // 2, turn // 4

        far = sum(bit << i for i, (bit, _) in enumerate(offsets))
        turn = sum(step << (2 * i) for i, (_, step) in enumerate(offsets))
        lax.fori_loop(0, 8, body, (jnp.int32(far), jnp.int32(turn)))

    def normed_rows(values):
        return values * lax.rsqrt(jnp.mean(values * values, axis=-1, keepdims=True) + EPSILON)

    def turned(values, rows):
        return values * cos_t[rows, :] + pltpu.roll(values, HD // 2, 1) * sin_t[rows, :]

    def project(rows):
        block = normed[rows, :]
        out = dot(block, w_all[...])
        raw[rows, :] = out[:, :384]
        for head in range(2):
            q_rows[head, rows, :] = turned(
                normed_rows(out[:, head * HD : (head + 1) * HD]) * query_gain[...], rows
            ).astype(BF16)
        k_rows[rows, :] = turned(normed_rows(out[:, 256:384]) * key_gain[...], rows).astype(BF16)
        v_rows[rows, :] = out[:, 384:].astype(BF16)
        normed_t[:, rows] = block.T

    def blocks_of_queries(start_at, width, work):
        def body(i, carry):
            head, at = i % 2, start_at + i // 2
            first_row = pl.multiple_of(at * QB, QB)
            work(head, first_row, pl.ds(first_row, QB), width)
            return carry

        lax.fori_loop(0, 4, body, 0)

    def forward(head, first_row, rows, width):
        scores = dot_t(q_rows[head, rows, :], k_rows[0:width, :]) * (SCALE * LOG2E)
        row_pos = first_row + lax.broadcasted_iota(jnp.int32, (QB, width), 0)
        col_pos = lax.broadcasted_iota(jnp.int32, (QB, width), 1)
        scores = jnp.where(col_pos <= row_pos, scores, MASKED)
        raised = jnp.exp2(scores - jnp.max(scores, axis=-1, keepdims=True))
        p = raised * (1.0 / jnp.sum(raised, axis=-1, keepdims=True))
        prob[head, rows, 0:width] = p
        out = dot(p.astype(BF16), v_rows[0:width, :]).astype(BF16)
        att_t[pl.ds(pl.multiple_of(head * HD, HD), HD), rows] = out.T

    def backward(head, first_row, rows, width):
        p = prob[head, rows, 0:width]
        up = d_att[head, rows, :]
        d_prob = dot_t(up, v_rows[0:width, :])
        centred = d_prob - jnp.sum(p * d_prob, axis=-1, keepdims=True)
        d_scores = (p * centred * SCALE).astype(BF16)
        d_values[0:width, :] += dot(p.astype(BF16).T, up)
        d_keys[0:width, :] += dot(d_scores.T, q_rows[head, rows, :])
        d_query = dot(d_scores, k_rows[0:width, :])
        cols = pl.ds(pl.multiple_of(head * HD, HD), HD)
        d_proj[rows, cols] = unshaped(d_query, raw[rows, cols], query_gain, rows)

    def unshaped(d_turned, before, gain, rows):
        d_grouped = d_turned * cos_t[rows, :] + pltpu.roll(d_turned * sin_t[rows, :], HD // 2, 1)
        d_norm = d_grouped * gain[...]
        inverse = lax.rsqrt(jnp.mean(before * before, axis=-1, keepdims=True) + EPSILON)
        inner = jnp.mean(before * d_norm, axis=-1, keepdims=True)
        return (inverse * d_norm - before * (inverse * inverse * inverse * inner)).astype(BF16)

    def upstream(rows):
        out = dot_t(cots[rows, :], wo[...]).astype(BF16)
        d_att[0, rows, :] = out[:, :HD]
        d_att[1, rows, :] = out[:, HD:]

    def pass_on_first():
        third(0)
        first(1)

    first(0)
    for name in ("wq", "wk", "wv", "cos", "sin", "cot"):
        loads[name].wait()
    over_blocks(
        order,
        {
            1: lambda: second(0),
            4: pass_on_first,
            5: lambda: got(0, XM, XP),
            7: lambda: got(0, X2A, X2B),
        },
        project,
    )
    second(1)
    blocks_of_queries(0, LEN // 2, forward)
    third(1)
    blocks_of_queries(2, LEN, forward)
    loads["wo"].wait()
    loads["lo"].wait()
    over_blocks(order, {5: lambda: got(1, XM, XP), 7: lambda: got(1, X2A, X2B)}, upstream)

    def exchanged(at, mine, theirs):
        return pltpu.make_async_remote_copy(
            src_ref=mine,
            dst_ref=theirs,
            send_sem=ex_send.at[at],
            recv_sem=ex_recv.at[at],
            device_id={"rep": ahead},
            device_id_type=MESH,
        )

    def exchanged_out(at):
        cols = pl.ds(pl.multiple_of(at * 512, 512), 512)
        return exchanged(at, moved_out.at[:, cols], partner_out.at[:, cols])

    def exchanged_in(at):
        rows = pl.ds(pl.multiple_of(at * 256, 256), 256)
        return exchanged(4 + at, moved.at[rows], partner.at[rows])

    def relay_first(at, mine):
        return pltpu.make_async_remote_copy(
            src_ref=mine,
            dst_ref=relay.at[at],
            send_sem=ex_send.at[4 * at + 3],
            recv_sem=relay_recv.at[at],
            device_id={"rep": via},
            device_id_type=MESH,
        )

    def relay_leg(at):
        return pltpu.make_async_remote_copy(
            src_ref=relay.at[at],
            dst_ref=partner_out.at[:, 1536:2048] if at == 0 else partner.at[1024 * at - 256 : 1024 * at],
            send_sem=relay_send.at[at],
            recv_sem=ex_recv.at[4 * at + 3],
            device_id={"rep": via_ahead},
            device_id_type=MESH,
        )

    def relay_on(at):
        if relayed:
            relay_first(at, relay.at[at]).wait_recv()
            relay_leg(at).start()

    def send_chunk(at, group, direct, mine):
        if relayed:
            pl.when(at % 4 != 3)(lambda: direct.start())
            pl.when(at % 4 == 3)(lambda: relay_first(group, mine).start())
        else:
            direct.start()

    def out_step(at, carry):
        cols = pl.ds(pl.multiple_of(at * 512, 512), 512)
        grad = dot(att_t[...], cots[:, cols])
        moved_out[:, cols] = (
            wo[:, cols].astype(F32)
            + MOMENTUM * lo[:, cols].astype(F32)
            - LEARNING_RATE * grad
        ).astype(BF16)
        send_chunk(at, 0, exchanged_out(at), moved_out.at[:, cols])
        return carry

    lax.fori_loop(0, 4, out_step, 0)
    d_keys[...] = jnp.zeros_like(d_keys)
    d_values[...] = jnp.zeros_like(d_values)
    blocks_of_queries(0, LEN // 2, backward)
    blocks_of_queries(2, LEN, backward)

    def key_step(at, carry):
        rows = pl.ds(pl.multiple_of(at * 256, 256), 256)
        d_proj[rows, 256:384] = unshaped(d_keys[rows, :], raw[rows, 256:384], key_gain, rows)
        d_proj[rows, 384:512] = d_values[rows, :].astype(BF16)
        return carry

    lax.fori_loop(0, 4, key_step, 0)

    relay_on(0)
    for which in range(2):
        for tag in plans:
            gather(which, tag).wait_send()

    terms = cots
    first_half, second_half = pl.ds(0, ROWS // 2), pl.ds(ROWS // 2, ROWS // 2)
    routes = {
        RC: (rows_of(hx, y2), arrived.at[0], t_x),
        RP: (rows_of(hx, yp), arrived.at[1], t_yp),
        RM: (rows_of(hx, ym), arrived.at[2], t_ym),
        HA: (half_of(h, y2, 0), arrived.at[3, first_half], t_ym),
        HB: (half_of(h, y2, 1), arrived.at[3, second_half], t_yp),
        NX: (rows_of(hx, y), arrived.at[6], t_x),
        NMA: (half_of(h, ym, 0), arrived.at[4, first_half], t_ym),
        NMB: (half_of(h, ym, 1), arrived.at[4, second_half], t_ym),
        NPA: (half_of(h, yp, 0), arrived.at[5, first_half], t_yp),
        NPB: (half_of(h, yp, 1), arrived.at[5, second_half], t_yp),
    }

    def scatter(tag):
        rows, dst, target = routes[tag]
        return pltpu.make_async_remote_copy(
            src_ref=terms.at[rows],
            dst_ref=dst,
            send_sem=rs_send.at[tag],
            recv_sem=rs_recv.at[tag],
            device_id={"tp": target},
            device_id_type=MESH,
        )

    def add(tag, *arrivals):
        rows = routes[tag][0]
        total = terms[rows, :].astype(F32)
        for arrival in arrivals:
            total = total + arrival.astype(F32)
        terms[rows, :] = total.astype(BF16)
        scatter(tag).start()

    def term(rows):
        terms[rows, :] = dot_t(d_proj[rows, :], w_all[...]).astype(BF16)

    over_blocks(
        order[::-1],
        {},
        term,
        {
            0: lambda: scatter(RC).start(),
            1: lambda: scatter(RP).start(),
            2: lambda: scatter(RM).start(),
            5: lambda: scatter(NPA).start(),
            6: lambda: scatter(NMB).start(),
        },
    )

    for name in ("lq", "lk", "lv"):
        loads[name].wait()

    def weight_step(at, carry):
        rows = pl.ds(pl.multiple_of(at * 256, 256), 256)
        grad = dot(normed_t[rows, :], d_proj[...])
        moved[rows, :] = (
            w_all[rows, :].astype(F32)
            + MOMENTUM * l_all[rows, :].astype(F32)
            - LEARNING_RATE * grad
        ).astype(BF16)
        send_chunk(at, 1 + at // 4, exchanged_in(at), moved.at[rows])
        return carry

    lax.fori_loop(0, 8, weight_step, 0)

    scatter(RC).wait_recv()
    add(HA, arrived[0, first_half, :])
    add(HB, arrived[0, second_half, :])
    scatter(RP).wait_recv()
    scatter(RM).wait_recv()
    add(NX, arrived[1], arrived[2])
    scatter(HA).wait_recv()
    add(NMA, arrived[3, first_half, :])
    scatter(HB).wait_recv()
    add(NPB, arrived[3, second_half, :])
    relay_on(1)
    for tag in (NMA, NMB, NPA, NPB, NX):
        scatter(tag).wait_recv()
    loads["cot2"].wait()

    def token_step(at, carry):
        rows = pl.ds(pl.multiple_of(at * 32, 32), 32)
        total = terms[pl.ds(pl.multiple_of(tp * ROWS + at * 32, 32), 32), :].astype(F32)
        for slot in range(4, 7):
            total = total + arrived[slot, rows, :].astype(F32)
        x = tok[rows, :].astype(F32)
        inverse = lax.rsqrt(jnp.mean(x * x, axis=-1, keepdims=True) + EPSILON)
        inner = jnp.mean(x * total, axis=-1, keepdims=True)
        tok[rows, :] = (
            inverse * total
            - x * (inverse * inverse * inverse * inner)
            + cot_own[rows, :].astype(F32)
        ).astype(BF16)
        return carry

    lax.fori_loop(0, ROWS // 32, token_step, 0)
    store_tokens = pltpu.make_async_copy(tok, o_tokens, store_sem.at[28])
    store_tokens.start()
    relay_on(2)

    def averaged(mine, theirs):
        return (0.5 * (mine.astype(F32) + theirs.astype(F32))).astype(BF16)

    def stored_out(at):
        cols = pl.ds(pl.multiple_of(at * 512, 512), 512)
        return (pltpu.make_async_copy(partner_out.at[:, cols], o_out.at[:, cols], store_sem.at[at]),)

    def stored_in(at):
        rows = pl.ds(pl.multiple_of(at * 256, 256), 256)
        return tuple(
            pltpu.make_async_copy(partner.at[rows, cols], out.at[rows], store_sem.at[4 + 3 * at + i])
            for i, (cols, out) in enumerate(
                ((pl.ds(0, 256), o_query), (pl.ds(256, 128), o_key), (pl.ds(384, 128), o_value))
            )
        )

    def average_out(at, carry):
        exchanged_out(at).wait_recv()
        cols = pl.ds(pl.multiple_of(at * 512, 512), 512)
        partner_out[:, cols] = averaged(moved_out[:, cols], partner_out[:, cols])
        for copy in stored_out(at):
            copy.start()
        return carry

    def average_in(at, carry):
        exchanged_in(at).wait_recv()
        rows = pl.ds(pl.multiple_of(at * 256, 256), 256)
        partner[rows, :] = averaged(moved[rows, :], partner[rows, :])
        for copy in stored_in(at):
            copy.start()
        return carry

    def finish_out(at, carry):
        exchanged_out(at).wait_send()
        for copy in stored_out(at):
            copy.wait()
        return carry

    def finish_in(at, carry):
        exchanged_in(at).wait_send()
        for copy in stored_in(at):
            copy.wait()
        return carry

    lax.fori_loop(0, 4, average_out, 0)
    lax.fori_loop(0, 8, average_in, 0)
    lax.fori_loop(0, 4, finish_out, 0)
    lax.fori_loop(0, 8, finish_in, 0)
    for tag in routes:
        scatter(tag).wait_send()
    if relayed:
        for at in range(3):
            relay_leg(at).wait_send()
    store_tokens.wait()


def training_step(exponent, arrays):
    def vmem(*shape, dtype=BF16):
        return pltpu.VMEM(shape, dtype)

    dma = pltpu.SemaphoreType.DMA
    any_spec = pl.BlockSpec(memory_space=pl.ANY)
    vmem_spec = pl.BlockSpec(memory_space=pltpu.VMEM)
    return pl.pallas_call(
        functools.partial(kernel, 1 << exponent),
        out_shape=(
            jax.ShapeDtypeStruct((COLS, 256), BF16),
            jax.ShapeDtypeStruct((COLS, 128), BF16),
            jax.ShapeDtypeStruct((COLS, 128), BF16),
            jax.ShapeDtypeStruct((256, COLS), BF16),
            jax.ShapeDtypeStruct((ROWS, COLS), BF16),
        ),
        in_specs=[any_spec] * 10 + [vmem_spec] * 2 + [any_spec] * 2,
        out_specs=(any_spec,) * 5,
        scratch_shapes=[
            vmem(ROWS, COLS),
            vmem(ROWS, COLS),
            vmem(LEN, COLS),
            vmem(LEN, COLS),
            vmem(COLS, LEN),
            vmem(COLS, QKV),
            vmem(COLS, QKV),
            vmem(QW, COLS),
            vmem(QW, COLS),
            vmem(LEN, HD, dtype=F32),
            vmem(LEN, HD, dtype=F32),
            vmem(LEN, 384, dtype=F32),
            vmem(2, LEN, HD),
            vmem(LEN, HD),
            vmem(LEN, HD),
            vmem(2, LEN, LEN, dtype=F32),
            vmem(QW, LEN),
            vmem(2, LEN, HD),
            vmem(LEN, HD, dtype=F32),
            vmem(LEN, HD, dtype=F32),
            vmem(LEN, QKV),
            vmem(7, ROWS, COLS),
            vmem(COLS, QKV),
            vmem(QW, COLS),
            vmem(COLS, QKV),
            vmem(QW, COLS),
            vmem(3, 256, 512),
            dma((13,)),
            dma((29,)),
            dma((2, 9)),
            dma((2, 9)),
            dma((10,)),
            dma((10,)),
            dma((12,)),
            dma((12,)),
            dma((3,)),
            dma((3,)),
        ],
        compiler_params=pltpu.CompilerParams(
            collective_id=exponent, has_side_effects=True, vmem_limit_bytes=60 << 20
        ),
        cost_estimate=pl.CostEstimate(
            flops=11_000_000_000, bytes_accessed=12_000_000, transcendentals=2_000_000
        ),
    )(*arrays)


def per_device(
    step_index, tokens, cotangent, w_query, w_key, w_value, w_out,
    last_query, last_key, last_value, last_out, query_gain, key_gain,
):
    levels = lax.axis_size("rep").bit_length() - 1
    cosine, sine = rope_tables(LEN)
    arrays = (
        tokens, cotangent, w_query[0], w_key[0], w_value[0], w_out[0],
        last_query[0], last_key[0], last_value[0], last_out[0],
        query_gain[None], key_gain[None], jnp.asarray(cosine), jnp.asarray(sine),
    )
    new_query, new_key, new_value, new_out, d_tokens = lax.switch(
        step_index[0] % levels,
        [functools.partial(training_step, exponent) for exponent in range(levels)],
        arrays,
    )
    return (new_query[None], new_key[None], new_value[None], new_out[None], d_tokens)


def solution(mesh):
    placed = (
        P(),
        P(("rep", "tp"), None),
        P(("rep", "tp"), None),
        P("rep", None, "tp"),
        P("rep", None, "tp"),
        P("rep", None, "tp"),
        P("rep", "tp", None),
        P("rep", None, "tp"),
        P("rep", None, "tp"),
        P("rep", None, "tp"),
        P("rep", "tp", None),
        P(),
        P(),
    )
    return jax.shard_map(
        per_device,
        mesh=mesh,
        in_specs=placed,
        out_specs=(
            P("rep", None, "tp"),
            P("rep", None, "tp"),
            P("rep", None, "tp"),
            P("rep", "tp", None),
            P(("rep", "tp"), None),
        ),
        check_vma=False,
    )
```

time: 234 us -> 216 us (0.923); the launches traced: 231 us -> 216 us
  loops' own time: 14.1 us -> 0.63 us
    another operation x1, loops' own time: 14.1 us -> 0.63 us  [per_device(): lax.switch(step_index[0] % levels, [functools.partial(training_step, expo...]
where the time goes in v2:
time: 216 us
  Pallas kernels  209 us (97%)
  local copies, waits for them, and re-layouts  4.98 us (2%)
    pallas_call x1, Pallas kernels, training_step(): pl.pallas_call(functools.partial(kernel, 1 << exponent), out_shape=(jax.S...  209 us
    unnamed x9, local copies, waits for them, and re-layouts  4.98 us

profile of v2, /device:TPU:2, one launch (start us, length us, event | category | flops | bytes accessed | tf_op | source)
XLA Modules:
  0.0 216.0 jit_solution(13408908187791212954)
XLA Ops:
  1.3 0.0 copy-start
  1.3 0.0 copy-start.1
  1.3 0.6 copy-done
  1.9 0.0 copy-done.1
  2.0 209.7 %conditional.1 = ((bf16[2048,256]{1,0:T(8,128)(2,1)S(1)}, bf16[2048,128]{1,0:T(8,128)(2,1)S(1)}, bf16[2048,128]{1,0:T(8,128)(2,1)S(1)}, bf16[256,2048]{1,0:T(8,128)(2,1)S(1)}, bf16[128,2048]{1,0:T(8,128)(2,1)S(1)})) conditional(s32[]{:T(128)} %clamp.3, (bf16[128,2048]{1,0:T(8,128)(2,1)}, bf16[128,2048]{1,0:T(8,128)(2,1)}, ...), branch_computations={%region_0.1_spmd, %region_1.2_spmd, %region_2.3_spmd, %region_3.4_... | conditional | flops 11000000512 | bytes 12000008 | solution.py:586
  2.0 209.1 %branch_3_fun.1 = (bf16[2048,256]{1,0:T(8,128)(2,1)S(1)}, bf16[2048,128]{1,0:T(8,128)(2,1)S(1)}, bf16[2048,128]{1,0:T(8,128)(2,1)S(1)}, bf16[256,2048]{1,0:T(8,128)(2,1)S(1)}, bf16[128,2048]{1,0:T(8,128)(2,1)S(1)}) custom-call(bf16[128,2048]{1,0:T(8,128)(2,1)} %get-tuple-element.217.tokens, bf16[128,2048]{1,0:T(8,128)(2,1)} %get-tuple-element.218.cotangent, ...), custom_call_target="tpu_custom_call" | custom-call | flops 11000000512 | bytes 12000000 | tf_op jit(solution)/shard_map/cond/branch_3_fun/pallas_call | solution.py:516
  211.7 1.0 copy.51
  212.6 0.8 copy.52
  213.4 0.8 copy.53
  214.2 1.0 copy.54
  215.2 0.8 copy.55
Async XLA Ops:
  1.3 0.7 copy-start
  1.3 0.7 copy-start.1
